TPU v7x, 32 devices: a whole 2x2x4 slice. The times are simulated.
32 devices in a mesh: seq: 16 (over z, y, x), head: 2 (over core).
Axes of the slice: x: 2, y: 2, z: 4, core: 2. Of those that a mesh axis runs over, the one named last changes fastest.
Arguments:
- queries: bfloat16 [16, 128, 576], P(None, 'head'), may hold values from -24 to 24
- cache: bfloat16 [16, 2048, 576], P(None, 'seq'), may hold values from -4 to 4
- block_ids: int32 [16, 32], replicated, may hold values from 0 to 31, as said below
- lengths: int32 [16], replicated, may hold values from 2048 to 2048, as said below
- value_up: bfloat16 [128, 512, 128], P('head'), may hold values from -2 to 2
- out_proj: bfloat16 [16384, 7168], P('head', 'seq'), may hold values from -0.046875 to 0.046875
Outputs:
- mixed: bfloat16 [16, 7168], P(None, 'seq')
Inputs may be any that keep to these rules, and one draw needn't show every extreme that they name: `block_ids`: each row's block numbers are distinct, each below ceil(lengths / 64), and include the row's last filled block. `lengths`: some row is full in every draw.
All inputs are finite; a program needn't handle non-finite values.
Results may differ from a plain program's by a relative error of at most 0.019.
Values may be sent and summed in bfloat16 or wider, within the bound.
A program may use at most 64 MiB of HBM per device.

v0:
```python
import jax
import jax.numpy as jnp
from jax import lax
from jax.sharding import PartitionSpec as P

BLOCK = 64


softmax_scale = 192.0 ** (-0.5)


def body(queries, cache, block_ids, lengths, value_up, out_proj):
    rows, span, width = cache.shape
    latent = value_up.shape[1]
    first = lax.axis_index("seq") * span
    position = first + jnp.arange(span, dtype=jnp.int32)
    chosen = jnp.any(block_ids[:, :, None] == (position // BLOCK)[None, None, :], axis=1)
    live = chosen & (position[None, :] < lengths[:, None])
    scores = (
        jnp.einsum("rhc,rsc->rhs", queries, cache, preferred_element_type=jnp.float32)
        * softmax_scale
    )
    masked = jnp.where(live[:, None, :], scores, -jnp.inf)
    local_top = jnp.max(masked, axis=-1)
    top = lax.pmax(local_top, "seq")
    expo = jnp.where(live[:, None, :], jnp.exp(masked - top[:, :, None]), jnp.float32(0.0))
    local_total = jnp.sum(expo, axis=-1)
    weights = expo.astype(jnp.bfloat16)
    summed = jnp.einsum(
        "rhs,rsc->rhc", weights, cache[:, :, :latent], preferred_element_type=jnp.float32
    )
    upward = value_up.astype(jnp.float32)
    total, summed_all = lax.psum((local_total, summed), "seq")
    context = summed_all / total[:, :, None]
    heads_out = jnp.einsum("rhc,hcv->rhv", context, upward, precision=lax.Precision.HIGHEST)
    flat = heads_out.astype(jnp.bfloat16).reshape(rows, -1)
    partial_out = jnp.dot(flat, out_proj, preferred_element_type=jnp.float32)
    return lax.psum(partial_out.astype(jnp.bfloat16), "head")


def solution(mesh):
    return jax.shard_map(
        body,
        mesh=mesh,
        in_specs=(
            P(None, "head", None),
            P(None, "seq", None),
            P(),
            P(),
            P("head", None, None),
            P("head", "seq"),
        ),
        out_specs=P(None, "seq"),
        check_vma=False,
    )
```

profile of v0, /device:TPU:0, one launch (start us, length us, event | category | flops | bytes accessed | tf_op | source)
XLA Modules:
  0.0 203.2 jit_solution(6820584401025848015)
XLA Ops:
  6.5 0.0 copy-start
  6.5 0.0 all-reduce.2.cloned.1.call-start
  6.6 0.9 compare_reduce_fusion
  7.5 0.7 compare_and_fusion
  8.2 0.0 copy-done
  8.2 2.3 %fusion.20 = (f32[16,64]{1,0:T(8,128)S(1)}, f32[16,64,128]{2,1,0:T(8,128)S(1)}) fusion(bf16[16,64,576]{2,1,0:T(8,128)(2,1)S(1)} %copy-done, bf16[16,128,576]{1,2,0:T(8,128)(2,1)} %param.7, pred[16,128]{1,0:T(8,128)(4,1)S(1)} %compare_and_fusion), kind=kOutput, calls=%fused_computation.26 | convolution fusion | flops 151387136 | bytes 4069376 | tf_op jit(solution)/shard_map/rhc,rsc->rhs/dot_general | solution.py:20
  10.6 44.0 %pmax.7 = f32[16,64]{1,0:T(8,128)S(1)} all-reduce(f32[16,64]{1,0:T(8,128)S(1)} %get-tuple-element.5), channel_id=1, replica_groups=mesh['seq'=16,'head'=2] {'seq'}, use_global_device_ids=true, to_apply=%region_2.3 | all-reduce | flops 1024 | bytes 8192 | tf_op jit(solution)/shard_map/pmax | solution.py:25
  54.6 3.8 %fusion.2 = f32[16,64,512]{2,1,0:T(8,128)} fusion(bf16[16,128,576]{1,2,0:T(8,128)(2,1)} %param.7, f32[16,64,128]{2,1,0:T(8,128)S(1)} %get-tuple-element.6, f32[16,64]{1,0:T(8,128)S(1)} %pmax.7, pred[16,128]{1,0:T(8,128)(4,1)S(1)} %compare_and_fusion), kind=kOutput, calls=%fused_computation.2 | convolution fusion | flops 134610944 | bytes 4724736 | tf_op jit(solution)/shard_map/rhs,rsc->rhc/dot_general | solution.py:29
  58.4 0.0 all-reduce.2.cloned.1.call-update
  58.4 0.4 fusion.11
  58.8 38.4 %psum.22 = f32[16,64]{1,0:T(8,128)S(1)} all-reduce(f32[16,64]{1,0:T(8,128)S(1)} %fusion.11), channel_id=1, replica_groups=mesh['seq'=16,'head'=2] {'seq'}, use_global_device_ids=true, to_apply=%region_5.6 | all-reduce | flops 1024 | bytes 8192 | tf_op jit(solution)/shard_map/psum | solution.py:33
  97.2 84.1 %all-reduce.2.cloned.1.call-done = f32[16,64,512]{2,1,0:T(8,128)} async-done(((f32[16,64,512]{2,1,0:T(8,128)}), f32[16,64,512]{2,1,0:T(8,128)}) %all-reduce.2.cloned.1.call-update) | async-done | bytes 2097168 | tf_op jit(solution)/shard_map/psum | solution.py:33
  181.4 0.0 slice-start
  181.4 1.9 broadcast_divide_fusion
  183.3 0.0 slice-start.1
  183.4 7.0 %fusion.8 = bf16[64,2,8,128]{3,2,1,0:T(8,128)(2,1)S(1)} fusion(bf16[64,512,128]{2,1,0:T(8,128)(2,1)} %param.10, f32[16,64,512]{2,1,0:T(8,128)S(1)} %broadcast_divide_fusion), kind=kOutput, calls=%fused_computation.7 | convolution fusion | flops 805437440 | bytes 10747904 | tf_op jit(solution)/shard_map/rhc,hcv->rhv/dot_general | solution.py:35
  190.4 0.0 slice-done
  190.4 0.0 slice-done.1
  190.4 2.0 convolution_convert_fusion
  192.4 4.0 %psum.23 = bf16[16,448]{1,0:T(8,128)(2,1)} all-reduce(bf16[16,448]{1,0:T(8,128)(2,1)S(1)} %convolution_convert_fusion), channel_id=1, replica_groups=mesh['seq'=16,'head'=2] {'head'}, use_global_device_ids=true, to_apply=%region_6.7 | all-reduce | flops 7168 | bytes 28672 | tf_op jit(solution)/shard_map/psum | solution.py:38
  (2 shorter events, 0.0 us)
Async XLA Ops:
  6.5 1.7 copy-start
  6.5 174.9 %all-reduce.2.cloned.1.call-start = ((), (), s32[]{:S(2)}) async-start(), calls=%async_computation | async-start | bytes 4194304 | tf_op jit(solution)/shard_map/psum | solution.py:33
  181.4 9.0 %slice-start = ((s8[7340032]{0:T(1024)(128)(4,1)}), s8[4194304]{0:T(1024)(128)(4,1)S(1)}, s32[]{:S(2)}) async-start(s8[7340032]{0:T(1024)(128)(4,1)} %bitcast.10), calls=%async_computation.1 | async-start | bytes 8388608
  183.3 7.0 %slice-start.1 = ((s8[7340032]{0:T(1024)(128)(4,1)}), s8[3145728]{0:T(1024)(128)(4,1)S(1)}, s32[]{:S(2)}) async-start(s8[7340032]{0:T(1024)(128)(4,1)} %bitcast.10), calls=%async_computation.2 | async-start | bytes 6291456
Sparse Core Ops, SparseCore 0:
  58.5 122.8 all-reduce.1
where the time goes:
time: 203 us
  blocking collectives  86.4 us (43%)
  waiting for transfers between devices  84.2 us (41%)
  matrix products  15.1 us (7%)
  between operations  13.5 us (7%)
  other arithmetic  4.03 us (2%)
    psum x1, waiting for transfers between devices, body(): total, summed_all = lax.psum((local_total, summed), 'seq')  84.1 us
    pmax x1, blocking collectives, body(): top = lax.pmax(local_top, 'seq')  44 us
    psum x1, blocking collectives, body(): total, summed_all = lax.psum((local_total, summed), 'seq')  38.4 us
    dot_general x1, matrix products, body(): jnp.einsum('rhc,hcv->rhv', context, upward, precision=lax.Precision.HIGHEST)  7 us
  transfers between devices with their start and end apart: 1, of which 1 were waited for; matrix products, arithmetic and copies ran while one was open for 0% of the time, Pallas kernels for 0%

commit v1 on v0

--- a/solution.py
+++ b/solution.py
@@ -1,15 +1,324 @@
+import functools
+
 import jax
 import jax.numpy as jnp
 from jax import lax
+from jax.experimental import pallas as pl
+from jax.experimental.pallas import tpu as pltpu
 from jax.sharding import PartitionSpec as P
 
 BLOCK = 64
+DEAD = -1e30
+MESH = pl.DeviceIdType.MESH
 
 
 softmax_scale = 192.0 ** (-0.5)
 
 
-def body(queries, cache, block_ids, lengths, value_up, out_proj):
+def kernel(
+    n,
+    n_head,
+    lengths_ref,
+    ids_ref,
+    q_hbm,
+    k_hbm,
+    v_hbm,
+    w_hbm,
+    out_ref,
+    q,
+    k,
+    v,
+    w,
+    scores,
+    summed,
+    stat_out,
+    stat_in,
+    spread,
+    part_out,
+    part_in,
+    flat,
+    group,
+    local_sem,
+    v_sem,
+    w_sem,
+    stat_send,
+    stat_recv,
+    part_send,
+    part_recv,
+    flat_send,
+    flat_recv,
+    group_send,
+    group_recv,
+):
+    rows, heads, width = q.shape
+    span = k.shape[2]
+    latent, vdim = v.shape[1:]
+    own = heads // n
+    tiles = latent // 128
+    piece = own * vdim
+    me = lax.axis_index("seq")
+    my_head = lax.axis_index("head")
+
+    def v_copy(t):
+        part = pl.ds(t * own, own)
+        return pltpu.make_async_copy(v_hbm.at[part], v.at[part], v_sem.at[t])
+
+    def w_copy(t):
+        part = pl.ds(pl.multiple_of(t * piece, piece), piece)
+        return pltpu.make_async_copy(w_hbm.at[:, part], w.at[t], w_sem.at[t])
+
+    q_copy = pltpu.make_async_copy(q_hbm, q, local_sem.at[0])
+    k_copy = pltpu.make_async_copy(k_hbm, k, local_sem.at[1])
+    q_copy.start()
+    k_copy.start()
+
+    barrier = pltpu.get_barrier_semaphore()
+
+    @pl.loop(1, n)
+    def _(i):
+        pl.semaphore_signal(
+            barrier, inc=1, device_id={"seq": lax.rem(me + i, n)}, device_id_type=MESH
+        )
+
+    for j in range(1, n_head):
+        pl.semaphore_signal(
+            barrier, inc=1, device_id={"head": lax.rem(my_head + j, n_head)}, device_id_type=MESH
+        )
+
+    @pl.loop(1, n + 1)
+    def _(i):
+        v_copy(lax.rem(me + i, n)).start()
+
+    @pl.loop(0, n)
+    def _(i):
+        w_copy(lax.rem(me + i, n)).start()
+
+    lane = lax.broadcasted_iota(jnp.int32, (rows, span), 1)
+    line = lax.broadcasted_iota(jnp.int32, (rows, span), 0)
+    first = me * span
+    ids = ids_ref[...]
+    chosen = jnp.zeros((rows, span), jnp.int32)
+    for b in range(span // BLOCK):
+        hit = jnp.max((ids == first // BLOCK + b).astype(jnp.int32), axis=1, keepdims=True)
+        chosen = jnp.where(lane // BLOCK == b, hit, chosen)
+    filled = jnp.zeros((rows, span), jnp.int32)
+    for r in range(rows):
+        filled = jnp.where(line == r, lengths_ref[r], filled)
+    live = jnp.where(first + lane < filled, chosen, 0).astype(jnp.float32)
+
+    q_copy.wait()
+    k_copy.wait()
+    for r in range(rows):
+        s = jnp.dot(q[r], k[r], preferred_element_type=jnp.float32) * softmax_scale
+        scores[r] = jnp.where(live[r : r + 1] > 0.0, s, DEAD)
+    stats = jnp.zeros((heads, 128), jnp.float32)
+    stat_lane = lax.broadcasted_iota(jnp.int32, (heads, 128), 1)
+    for r in range(rows):
+        s = scores[r]
+        top = jnp.max(s, axis=1, keepdims=True)
+        expo = jnp.where(live[r : r + 1] > 0.0, jnp.exp(s - top), 0.0)
+        total = jnp.sum(expo, axis=1, keepdims=True)
+        some = total > 0.0
+        total = jnp.where(some, total, 1.0)
+        stats = jnp.where(stat_lane == r, jnp.where(some, top + jnp.log(total), DEAD), stats)
+        out = lax.dot_general(
+            expo.astype(jnp.bfloat16),
+            k[r, :latent, :],
+            (((1,), (1,)), ((), ())),
+            preferred_element_type=jnp.float32,
+        )
+        out = out * (1.0 / total)
+        for c in range(tiles):
+            summed[c, r * heads : (r + 1) * heads, :] = out[:, c * 128 : (c + 1) * 128]
+    for t in range(n):
+        stat_out[t] = stats[t * own : (t + 1) * own]
+
+    pl.semaphore_wait(barrier, n - 1 + n_head - 1)
+
+    def stat_copy(t, slot):
+        return pltpu.make_async_remote_copy(
+            src_ref=stat_out.at[t],
+            dst_ref=stat_in.at[slot],
+            send_sem=stat_send.at[t],
+            recv_sem=stat_recv.at[slot],
+            device_id={"seq": t},
+            device_id_type=MESH,
+        )
+
+    def part_copy(t, slot):
+        return pltpu.make_async_remote_copy(
+            src_ref=part_out.at[t],
+            dst_ref=part_in.at[slot],
+            send_sem=part_send.at[t],
+            recv_sem=part_recv.at[slot],
+            device_id={"seq": t},
+            device_id_type=MESH,
+        )
+
+    def flat_copy(t, slot):
+        return pltpu.make_async_remote_copy(
+            src_ref=flat.at[slot],
+            dst_ref=flat.at[slot],
+            send_sem=flat_send.at[t],
+            recv_sem=flat_recv.at[slot],
+            device_id={"seq": t},
+            device_id_type=MESH,
+        )
+
+    @pl.loop(1, n)
+    def _(i):
+        stat_copy(lax.rem(me + i, n), me).start()
+
+    def project(t, dst):
+        v_copy(t).wait()
+        for j in range(own):
+            h = t * own + j
+            x = jnp.concatenate(
+                [summed[c, pl.ds(h, rows, stride=heads), :] for c in range(tiles)], axis=1
+            )
+            y = jnp.dot(x.astype(jnp.bfloat16), v[h], preferred_element_type=jnp.float32)
+            dst[j] = y.astype(jnp.bfloat16)
+
+    @pl.loop(1, n)
+    def _(i):
+        t = lax.rem(me + i, n)
+        project(t, part_out.at[t])
+        part_copy(t, me).start()
+
+    project(me, part_in.at[me])
+    stat_in[me] = stat_out[me]
+
+    @pl.loop(1, n)
+    def _(i):
+        stat_copy(me, lax.rem(me + n - i, n)).wait_recv()
+
+    got = [stat_in[d] for d in range(n)]
+    best = functools.reduce(jnp.maximum, got)
+    got = [jnp.exp(g - best) for g in got]
+    scale = 1.0 / functools.reduce(jnp.add, got)
+    for d in range(n):
+        spread[d * own : (d + 1) * own, :] = got[d] * scale
+    share = jnp.transpose(spread[...])[:rows]
+
+    @pl.loop(1, n)
+    def _(i):
+        part_copy(me, lax.rem(me + n - i, n)).wait_recv()
+
+    for j in range(own):
+        y = jnp.zeros((rows, vdim), jnp.float32)
+        for d in range(n):
+            at = d * own + j
+            y = y + share[:, at : at + 1] * part_in[d, j].astype(jnp.float32)
+        flat[me, :, j * vdim : (j + 1) * vdim] = y.astype(jnp.bfloat16)
+
+    @pl.loop(1, n)
+    def _(i):
+        flat_copy(lax.rem(me + i, n), me).start()
+
+    def multiply(t):
+        w_copy(t).wait()
+        return lax.dot_general(
+            flat[t], w[t], (((1,), (1,)), ((), ())), preferred_element_type=jnp.float32
+        )
+
+    def step(i, total):
+        t = lax.rem(me + n - i, n)
+        flat_copy(me, t).wait_recv()
+        return total + multiply(t)
+
+    total = lax.fori_loop(1, n, step, multiply(me))
+    group[my_head] = total.astype(jnp.bfloat16)
+
+    def group_copy(to, slot):
+        return pltpu.make_async_remote_copy(
+            src_ref=group.at[slot],
+            dst_ref=group.at[slot],
+            send_sem=group_send.at[to],
+            recv_sem=group_recv.at[slot],
+            device_id={"head": to},
+            device_id_type=MESH,
+        )
+
+    for j in range(1, n_head):
+        group_copy(lax.rem(my_head + j, n_head), my_head).start()
+    for j in range(1, n_head):
+        group_copy(my_head, lax.rem(my_head + j, n_head)).wait_recv()
+    mixed = group[0].astype(jnp.float32)
+    for g in range(1, n_head):
+        mixed = mixed + group[g].astype(jnp.float32)
+    out_ref[...] = mixed.astype(jnp.bfloat16)
+
+    @pl.loop(1, n)
+    def _(i):
+        t = lax.rem(me + i, n)
+        stat_copy(t, me).wait_send()
+        part_copy(t, me).wait_send()
+        flat_copy(t, me).wait_send()
+
+    for j in range(1, n_head):
+        group_copy(lax.rem(my_head + j, n_head), my_head).wait_send()
+
+
+def fused(n, n_head, queries, cache, block_ids, lengths, value_up, out_proj):
+    rows, heads, width = queries.shape
+    span = cache.shape[1]
+    latent, vdim = value_up.shape[1:]
+    columns = out_proj.shape[1]
+    own = heads // n
+    dma = pltpu.SemaphoreType.DMA
+    any_space = pl.BlockSpec(memory_space=pl.ANY)
+    return pl.pallas_call(
+        functools.partial(kernel, n, n_head),
+        out_shape=jax.ShapeDtypeStruct((rows, columns), jnp.bfloat16),
+        in_specs=[
+            pl.BlockSpec(memory_space=pltpu.SMEM),
+            pl.BlockSpec(memory_space=pltpu.VMEM),
+            any_space,
+            any_space,
+            any_space,
+            any_space,
+        ],
+        out_specs=pl.BlockSpec(memory_space=pltpu.VMEM),
+        scratch_shapes=[
+            pltpu.VMEM((rows, heads, width), jnp.bfloat16),
+            pltpu.VMEM((rows, width, span), jnp.bfloat16),
+            pltpu.VMEM((heads, latent, vdim), jnp.bfloat16),
+            pltpu.VMEM((n, columns, own * vdim), jnp.bfloat16),
+            pltpu.VMEM((rows, heads, span), jnp.float32),
+            pltpu.VMEM((latent // 128, rows * heads, 128), jnp.float32),
+            pltpu.VMEM((n, own, 128), jnp.float32),
+            pltpu.VMEM((n, own, 128), jnp.float32),
+            pltpu.VMEM((heads, 128), jnp.float32),
+            pltpu.VMEM((n, own, rows, vdim), jnp.bfloat16),
+            pltpu.VMEM((n, own, rows, vdim), jnp.bfloat16),
+            pltpu.VMEM((n, rows, own * vdim), jnp.bfloat16),
+            pltpu.VMEM((n_head, rows, columns), jnp.bfloat16),
+            dma((2,)),
+            dma((n,)),
+            dma((n,)),
+            dma((n,)),
+            dma((n,)),
+            dma((n,)),
+            dma((n,)),
+            dma((n,)),
+            dma((n,)),
+            dma((n_head,)),
+            dma((n_head,)),
+        ],
+        compiler_params=pltpu.CompilerParams(
+            collective_id=0, has_side_effects=True, vmem_limit_bytes=60 * 2**20
+        ),
+    )(
+        lengths,
+        block_ids,
+        queries,
+        jnp.transpose(cache, (0, 2, 1)),
+        value_up,
+        jnp.transpose(out_proj),
+    )
+
+
+def spread_body(queries, cache, block_ids, lengths, value_up, out_proj):
     rows, span, width = cache.shape
     latent = value_up.shape[1]
     first = lax.axis_index("seq") * span
@@ -38,9 +347,16 @@
     return lax.psum(partial_out.astype(jnp.bfloat16), "head")
 
 
+def body(n, n_head, *args):
+    heads, span = args[0].shape[1], args[1].shape[1]
+    if heads % n or span % BLOCK or span % 128:
+        return spread_body(*args)
+    return fused(n, n_head, *args)
+
+
 def solution(mesh):
     return jax.shard_map(
-        body,
+        functools.partial(body, mesh.shape["seq"], mesh.shape["head"]),
         mesh=mesh,
         in_specs=(
             P(None, "head", None),

time: 203 us -> 30.5 us (0.15)
  blocking collectives: 86.4 us -> 0 us
  waiting for transfers between devices: 84.2 us -> 0 us
  Pallas kernels: 0 us -> 28.8 us
  matrix products: 15.1 us -> 0 us
  between operations: 13.5 us -> 0.01 us
  other arithmetic: 4.03 us -> 0 us
    psum x1 -> x0, waiting for transfers between devices: 84.1 us -> none  [body(): total, summed_all = lax.psum((local_total, summed), 'seq')]
    pmax x1 -> x0, blocking collectives: 44 us -> none  [body(): top = lax.pmax(local_top, 'seq')]
    psum x2 -> x0, blocking collectives: 42.4 us -> none  [the longest x1 38.4 us: body(): total, summed_all = lax.psum((local_total, summed), 'seq')]
    pallas_call x0 -> x1, Pallas kernels: none -> 28.8 us  [fused(): pl.pallas_call(functools.partial(kernel, n, n_head), out_shape=jax.ShapeD...]
    dot_general x4 -> x0, matrix products: 15.1 us -> none  [the longest x1 7 us: body(): jnp.einsum('rhc,hcv->rhv', context, upward, precision=lax.Precision.HIGHEST)]
  transfers between devices with their start and end apart: 1 -> 0, of which waited for: 1 -> 0; matrix products, arithmetic and copies ran while one was open for 0% -> 0% of each run, Pallas kernels for 0% -> 0%
where the time goes in v1:
time: 30.5 us; the launch traced here: 30.2 us
  Pallas kernels  28.8 us (94%)
  local copies, waits for them, and re-layouts  1.32 us (4%)
    pallas_call x1, Pallas kernels, fused(): pl.pallas_call(functools.partial(kernel, n, n_head), out_shape=jax.ShapeD...  28.8 us
    unnamed x1, local copies, waits for them, and re-layouts  1.32 us

profile of v1, /device:TPU:0, one launch (start us, length us, event | category | flops | bytes accessed | tf_op | source)
XLA Modules:
  0.0 30.2 jit_solution(8926682694923658802)
XLA Ops:
  0.0 28.8 %shard_map.64 = bf16[16,448]{1,0:T(8,128)(2,1)} custom-call(s32[16]{0:T(128)} %lengths_ref.1, s32[16,32]{1,0:T(8,128)} %ids_ref.1, bf16[16,64,576]{2,1,0:T(8,128)(2,1)} %q_hbm.1, bf16[16,576,128]{2,1,0:T(8,128)(2,1)} %bitcast.3, bf16[64,512,128]{2,1,0:T(8,128)(2,1)} %v_hbm.1, bf16[448,8192]{1,0:T(8,128)(2,1)} %bitcast.2), custom_call_target="tpu_custom_call" | custom-call | tf_op jit(solution)/shard_map/pallas_call | solution.py:270
  28.8 1.3 %copy.8 = bf16[16,448]{1,0:T(8,128)(2,1)} copy(bf16[16,448]{1,0:T(8,128)(2,1)} %shard_map.64) | data formatting | bytes 28672

commit v2 on v1

--- a/solution.py
+++ b/solution.py
@@ -9,6 +9,7 @@
 
 BLOCK = 64
 DEAD = -1e30
+GROUPS = 4
 MESH = pl.DeviceIdType.MESH
 
 
@@ -67,10 +68,27 @@
         part = pl.ds(pl.multiple_of(t * piece, piece), piece)
         return pltpu.make_async_copy(w_hbm.at[:, part], w.at[t], w_sem.at[t])
 
-    q_copy = pltpu.make_async_copy(q_hbm, q, local_sem.at[0])
-    k_copy = pltpu.make_async_copy(k_hbm, k, local_sem.at[1])
-    q_copy.start()
-    k_copy.start()
+    def first_copies(g):
+        part = pl.ds(g * (rows // GROUPS), rows // GROUPS)
+        return (
+            pltpu.make_async_copy(q_hbm.at[part], q.at[part], local_sem.at[0, g]),
+            pltpu.make_async_copy(k_hbm.at[part], k.at[part], local_sem.at[1, g]),
+        )
+
+    for g in range(GROUPS):
+        for copy in first_copies(g):
+            copy.start()
+
+    half = n // 2
+    side = me // half
+    place = lax.rem(me, half)
+    mirror = (1 - side) * half + place
+
+    def near(i):
+        return side * half + lax.rem(place + i, half)
+
+    def far(i):
+        return (1 - side) * half + lax.rem(place + i, half)
 
     barrier = pltpu.get_barrier_semaphore()
 
@@ -84,14 +102,6 @@
         pl.semaphore_signal(
             barrier, inc=1, device_id={"head": lax.rem(my_head + j, n_head)}, device_id_type=MESH
         )
-
-    @pl.loop(1, n + 1)
-    def _(i):
-        v_copy(lax.rem(me + i, n)).start()
-
-    @pl.loop(0, n)
-    def _(i):
-        w_copy(lax.rem(me + i, n)).start()
 
     lane = lax.broadcasted_iota(jnp.int32, (rows, span), 1)
     line = lax.broadcasted_iota(jnp.int32, (rows, span), 0)
@@ -106,11 +116,21 @@
         filled = jnp.where(line == r, lengths_ref[r], filled)
     live = jnp.where(first + lane < filled, chosen, 0).astype(jnp.float32)
 
-    q_copy.wait()
-    k_copy.wait()
     for r in range(rows):
+        if r % (rows // GROUPS) == 0:
+            for copy in first_copies(r // (rows // GROUPS)):
+                copy.wait()
         s = jnp.dot(q[r], k[r], preferred_element_type=jnp.float32) * softmax_scale
         scores[r] = jnp.where(live[r : r + 1] > 0.0, s, DEAD)
+
+    @pl.loop(0, half)
+    def _(i):
+        v_copy(far(i)).start()
+
+    @pl.loop(1, half + 1)
+    def _(i):
+        v_copy(near(i)).start()
+
     stats = jnp.zeros((heads, 128), jnp.float32)
     stat_lane = lax.broadcasted_iota(jnp.int32, (heads, 128), 1)
     for r in range(rows):
@@ -155,11 +175,11 @@
             device_id_type=MESH,
         )
 
-    def flat_copy(t, slot):
+    def flat_copy(t, slot, sem):
         return pltpu.make_async_remote_copy(
             src_ref=flat.at[slot],
             dst_ref=flat.at[slot],
-            send_sem=flat_send.at[t],
+            send_sem=flat_send.at[sem],
             recv_sem=flat_recv.at[slot],
             device_id={"seq": t},
             device_id_type=MESH,
@@ -169,8 +189,15 @@
     def _(i):
         stat_copy(lax.rem(me + i, n), me).start()
 
+    @pl.loop(0, half)
+    def _(i):
+        w_copy(near(i)).start()
+
+    @pl.loop(0, half)
+    def _(i):
+        w_copy(far(i)).start()
+
     def project(t, dst):
-        v_copy(t).wait()
         for j in range(own):
             h = t * own + j
             x = jnp.concatenate(
@@ -179,12 +206,27 @@
             y = jnp.dot(x.astype(jnp.bfloat16), v[h], preferred_element_type=jnp.float32)
             dst[j] = y.astype(jnp.bfloat16)
 
-    @pl.loop(1, n)
-    def _(i):
-        t = lax.rem(me + i, n)
-        project(t, part_out.at[t])
-        part_copy(t, me).start()
-
+    def project_pair(t0, t1):
+        v_copy(t0).wait()
+        v_copy(t1).wait()
+        project(t0, part_out.at[t0])
+        project(t1, part_out.at[t1])
+        part_copy(t0, me).start()
+        part_copy(t1, me).start()
+
+    @pl.loop(0, half // 2)
+    def _(i):
+        project_pair(far(2 * i), far(2 * i + 1))
+
+    @pl.loop(0, half // 2 - 1)
+    def _(i):
+        project_pair(near(2 * i + 1), near(2 * i + 2))
+
+    last = near(half - 1)
+    v_copy(last).wait()
+    v_copy(me).wait()
+    project(last, part_out.at[last])
+    part_copy(last, me).start()
     project(me, part_in.at[me])
     stat_in[me] = stat_out[me]
 
@@ -211,9 +253,11 @@
             y = y + share[:, at : at + 1] * part_in[d, j].astype(jnp.float32)
         flat[me, :, j * vdim : (j + 1) * vdim] = y.astype(jnp.bfloat16)
 
-    @pl.loop(1, n)
-    def _(i):
-        flat_copy(lax.rem(me + i, n), me).start()
+    flat_copy(mirror, me, mirror).start()
+
+    @pl.loop(1, half)
+    def _(i):
+        flat_copy(near(i), me, near(i)).start()
 
     def multiply(t):
         w_copy(t).wait()
@@ -221,12 +265,25 @@
             flat[t], w[t], (((1,), (1,)), ((), ())), preferred_element_type=jnp.float32
         )
 
-    def step(i, total):
-        t = lax.rem(me + n - i, n)
-        flat_copy(me, t).wait_recv()
-        return total + multiply(t)
-
-    total = lax.fori_loop(1, n, step, multiply(me))
+    total = multiply(me)
+    flat_copy(me, mirror, mirror).wait_recv()
+
+    @pl.loop(1, half)
+    def _(i):
+        flat_copy(near(i), mirror, far(i)).start()
+
+    total = total + multiply(mirror)
+
+    def step(at):
+        def one(i, total):
+            t = at(half - i)
+            flat_copy(me, t, t).wait_recv()
+            return total + multiply(t)
+
+        return one
+
+    total = lax.fori_loop(1, half, step(near), total)
+    total = lax.fori_loop(1, half, step(far), total)
     group[my_head] = total.astype(jnp.bfloat16)
 
     def group_copy(to, slot):
@@ -243,17 +300,14 @@
         group_copy(lax.rem(my_head + j, n_head), my_head).start()
     for j in range(1, n_head):
         group_copy(my_head, lax.rem(my_head + j, n_head)).wait_recv()
-    mixed = group[0].astype(jnp.float32)
-    for g in range(1, n_head):
-        mixed = mixed + group[g].astype(jnp.float32)
-    out_ref[...] = mixed.astype(jnp.bfloat16)
+    out_ref[...] = group[...]
 
     @pl.loop(1, n)
     def _(i):
         t = lax.rem(me + i, n)
         stat_copy(t, me).wait_send()
         part_copy(t, me).wait_send()
-        flat_copy(t, me).wait_send()
+        flat_copy(t, me, t).wait_send()
 
     for j in range(1, n_head):
         group_copy(lax.rem(my_head + j, n_head), my_head).wait_send()
@@ -267,9 +321,9 @@
     own = heads // n
     dma = pltpu.SemaphoreType.DMA
     any_space = pl.BlockSpec(memory_space=pl.ANY)
-    return pl.pallas_call(
+    groups = pl.pallas_call(
         functools.partial(kernel, n, n_head),
-        out_shape=jax.ShapeDtypeStruct((rows, columns), jnp.bfloat16),
+        out_shape=jax.ShapeDtypeStruct((n_head, rows, columns), jnp.bfloat16),
         in_specs=[
             pl.BlockSpec(memory_space=pltpu.SMEM),
             pl.BlockSpec(memory_space=pltpu.VMEM),
@@ -293,7 +347,7 @@
             pltpu.VMEM((n, own, rows, vdim), jnp.bfloat16),
             pltpu.VMEM((n, rows, own * vdim), jnp.bfloat16),
             pltpu.VMEM((n_head, rows, columns), jnp.bfloat16),
-            dma((2,)),
+            dma((2, GROUPS)),
             dma((n,)),
             dma((n,)),
             dma((n,)),
@@ -316,6 +370,7 @@
         value_up,
         jnp.transpose(out_proj),
     )
+    return jnp.sum(groups.astype(jnp.float32), axis=0).astype(jnp.bfloat16)
 
 
 def spread_body(queries, cache, block_ids, lengths, value_up, out_proj):
@@ -349,7 +404,7 @@
 
 def body(n, n_head, *args):
     heads, span = args[0].shape[1], args[1].shape[1]
-    if heads % n or span % BLOCK or span % 128:
+    if heads % n or n % 4 or span % BLOCK or span % 128:
         return spread_body(*args)
     return fused(n, n_head, *args)
 

time: 30.5 us -> 29.2 us (0.957)
  other arithmetic: 0 us -> 1.38 us
  local copies, waits for them, and re-layouts: 1.32 us -> 0 us
  Pallas kernels: 28.8 us -> 27.6 us
    reduce_sum x0 -> x1, other arithmetic: none -> 1.38 us  [fused(): return jnp.sum(groups.astype(jnp.float32), axis=0).astype(jnp.bfloat16)]
    unnamed x1 -> x0, local copies, waits for them, and re-layouts: 1.32 us -> none
    pallas_call x1, Pallas kernels: 28.8 us -> 27.6 us  [fused(): pl.pallas_call(functools.partial(kernel, n, n_head), out_shape=jax.ShapeD...]
where the time goes in v2:
time: 29.2 us; the launch traced here: 29 us
  Pallas kernels  27.6 us (95%)
  other arithmetic  1.38 us (5%)
    pallas_call x1, Pallas kernels, fused(): pl.pallas_call(functools.partial(kernel, n, n_head), out_shape=jax.ShapeD...  27.6 us
    reduce_sum x1, other arithmetic, fused(): return jnp.sum(groups.astype(jnp.float32), axis=0).astype(jnp.bfloat16)  1.38 us

profile of v2, /device:TPU:0, one launch (start us, length us, event | category | flops | bytes accessed | tf_op | source)
XLA Modules:
  0.0 29.0 jit_solution(5241744349252534389)
XLA Ops:
  0.0 27.6 %shard_map.64 = bf16[2,16,448]{2,1,0:T(8,128)(2,1)} custom-call(s32[16]{0:T(128)} %lengths_ref.1, s32[16,32]{1,0:T(8,128)} %ids_ref.1, bf16[16,64,576]{2,1,0:T(8,128)(2,1)} %q_hbm.1, bf16[16,576,128]{2,1,0:T(8,128)(2,1)} %bitcast.3, bf16[64,512,128]{2,1,0:T(8,128)(2,1)} %v_hbm.1, bf16[448,8192]{1,0:T(8,128)(2,1)} %bitcast.2), custom_call_target="tpu_custom_call" | custom-call | tf_op jit(solution)/shard_map/pallas_call | solution.py:324
  27.6 1.4 %reduce_sum.12 = bf16[16,448]{1,0:T(8,128)(2,1)} reduce(bf16[2,16,448]{2,1,0:T(8,128)(2,1)} %shard_map.64, bf16[]{:T(256)} %constant.2.clone.1), dimensions={0}, to_apply=%region_0.0 | reduce | flops 7168 | bytes 43010 | tf_op jit(solution)/shard_map/reduce_sum | solution.py:373

commit v3 on v1

v3 whole, which is shorter than its diff:
```python
import functools

import jax
import jax.numpy as jnp
from jax import lax
from jax.experimental import pallas as pl
from jax.experimental.pallas import tpu as pltpu
from jax.sharding import PartitionSpec as P

BLOCK = 64
DEAD = -1e30
GROUPS = 4
MESH = pl.DeviceIdType.MESH


softmax_scale = 192.0 ** (-0.5)


def kernel(
    n,
    n_head,
    lengths_ref,
    ids_ref,
    q_hbm,
    k_hbm,
    v_hbm,
    w_hbm,
    out_ref,
    q,
    k,
    v,
    w,
    scores,
    summed,
    stat_out,
    stat_in,
    spread,
    part_out,
    part_in,
    flat,
    group,
    local_sem,
    v_sem,
    w_sem,
    stat_send,
    stat_recv,
    part_send,
    part_recv,
    flat_send,
    flat_recv,
    group_send,
    group_recv,
):
    rows, heads, width = q.shape
    span = k.shape[2]
    latent, vdim = v.shape[1:]
    own = heads // n
    tiles = latent // 128
    piece = own * vdim
    me = lax.axis_index("seq")
    my_head = lax.axis_index("head")
    half = n // 2
    pairs = half // 2
    some_heads = heads // 2
    side = me // half
    place = lax.rem(me, half)
    mirror = (1 - side) * half + place

    def near(i):
        return side * half + lax.rem(place + i, half)

    def first_copies(g):
        part = pl.ds(g * (rows // GROUPS), rows // GROUPS)
        return (
            pltpu.make_async_copy(q_hbm.at[part], q.at[part], local_sem.at[0, g]),
            pltpu.make_async_copy(k_hbm.at[part], k.at[part], local_sem.at[1, g]),
        )

    def v_copy(pair):
        part = pl.ds(pair * (2 * own), 2 * own)
        return pltpu.make_async_copy(v_hbm.at[part], v.at[part], v_sem.at[pair])

    def w_copy(at):
        part = pl.ds(pl.multiple_of(at * (half * piece), half * piece), half * piece)
        return pltpu.make_async_copy(w_hbm.at[:, part], w.at[at], w_sem.at[at])

    def pair_at(other, i):
        return other * pairs + lax.rem(place // 2 + 1 + i, pairs)

    for g in range(GROUPS):
        for copy in first_copies(g):
            copy.start()

    barrier = pltpu.get_barrier_semaphore()

    @pl.loop(1, n)
    def _(i):
        pl.semaphore_signal(
            barrier, inc=1, device_id={"seq": lax.rem(me + i, n)}, device_id_type=MESH
        )

    for j in range(1, n_head):
        pl.semaphore_signal(
            barrier, inc=1, device_id={"head": lax.rem(my_head + j, n_head)}, device_id_type=MESH
        )

    lane = lax.broadcasted_iota(jnp.int32, (rows, span), 1)
    line = lax.broadcasted_iota(jnp.int32, (rows, span), 0)
    first = me * span
    ids = ids_ref[...]
    chosen = jnp.zeros((rows, span), jnp.int32)
    for b in range(span // BLOCK):
        hit = jnp.max((ids == first // BLOCK + b).astype(jnp.int32), axis=1, keepdims=True)
        chosen = jnp.where(lane // BLOCK == b, hit, chosen)
    filled = jnp.zeros((rows, span), jnp.int32)
    for r in range(rows):
        filled = jnp.where(line == r, lengths_ref[r], filled)
    live = jnp.where(first + lane < filled, chosen, 0).astype(jnp.float32)

    def stat_copy(t):
        return pltpu.make_async_remote_copy(
            src_ref=stat_out.at[t],
            dst_ref=stat_in.at[me],
            send_sem=stat_send,
            recv_sem=stat_recv,
            device_id={"seq": t},
            device_id_type=MESH,
        )

    def part_copy(t):
        return pltpu.make_async_remote_copy(
            src_ref=part_out.at[t],
            dst_ref=part_in.at[me],
            send_sem=part_send,
            recv_sem=part_recv,
            device_id={"seq": t},
            device_id_type=MESH,
        )

    def flat_copy(t, slot, sem):
        return pltpu.make_async_remote_copy(
            src_ref=flat.at[slot],
            dst_ref=flat.at[slot],
            send_sem=flat_send,
            recv_sem=flat_recv.at[sem],
            device_id={"seq": t},
            device_id_type=MESH,
        )

    def several(ref, count, send_sem, recv_sem):
        part = ref.at[pl.ds(0, count)]
        return pltpu.make_async_remote_copy(
            src_ref=part,
            dst_ref=part,
            send_sem=send_sem,
            recv_sem=recv_sem,
            device_id={"seq": mirror},
            device_id_type=MESH,
        )

    def attend(other, opening):
        at = pl.multiple_of(other * some_heads, some_heads)
        for r in range(rows):
            if opening and r % (rows // GROUPS) == 0:
                for copy in first_copies(r // (rows // GROUPS)):
                    copy.wait()
            s = jnp.dot(
                q[r, pl.ds(at, some_heads), :], k[r], preferred_element_type=jnp.float32
            )
            scores[r] = jnp.where(live[r : r + 1] > 0.0, s * softmax_scale, DEAD)
        if opening:
            for i in range(pairs):
                v_copy(pair_at(other, i)).start()
            for i in range(pairs):
                v_copy(pair_at(1 - other, i)).start()
            w_copy(side).start()
            w_copy(1 - side).start()
        stats = jnp.zeros((some_heads, 128), jnp.float32)
        stat_lane = lax.broadcasted_iota(jnp.int32, (some_heads, 128), 1)
        for r in range(rows):
            s = scores[r]
            top = jnp.max(s, axis=1, keepdims=True)
            expo = jnp.where(live[r : r + 1] > 0.0, jnp.exp(s - top), 0.0)
            total = jnp.sum(expo, axis=1, keepdims=True)
            some = total > 0.0
            total = jnp.where(some, total, 1.0)
            stats = jnp.where(stat_lane == r, jnp.where(some, top + jnp.log(total), DEAD), stats)
            out = lax.dot_general(
                expo.astype(jnp.bfloat16),
                k[r, :latent, :],
                (((1,), (1,)), ((), ())),
                preferred_element_type=jnp.float32,
            )
            out = out * (1.0 / total)
            for c in range(tiles):
                summed[c, r * some_heads : (r + 1) * some_heads, :] = out[
                    :, c * 128 : (c + 1) * 128
                ]
        for t in range(half):
            stat_out[other * half + t] = stats[t * own : (t + 1) * own]

    def project(other, pair):
        v_copy(pair).wait()
        for j in range(2 * own):
            h = pair * (2 * own) + j
            x = jnp.concatenate(
                [
                    summed[c, pl.ds(h - other * some_heads, rows, stride=some_heads), :]
                    for c in range(tiles)
                ],
                axis=1,
            )
            y = jnp.dot(x.astype(jnp.bfloat16), v[h], preferred_element_type=jnp.float32)
            part_out[2 * pair + j // own, j % own] = y.astype(jnp.bfloat16)

    attend(1 - side, True)
    pl.semaphore_wait(barrier, n - 1 + n_head - 1)

    @pl.loop(0, pairs)
    def _(i):
        pair = pair_at(1 - side, i)
        project(1 - side, pair)
        for t in (2 * pair, 2 * pair + 1):
            part_copy(t).start()
            stat_copy(t).start()

    attend(side, False)

    @pl.loop(0, pairs - 1)
    def _(i):
        pair = pair_at(side, i)
        project(side, pair)
        for t in (2 * pair, 2 * pair + 1):
            part_copy(t).start()
            stat_copy(t).start()

    project(side, me // 2)
    beside = me // 2 * 2 + 1 - lax.rem(me, 2)
    part_copy(beside).start()
    stat_copy(beside).start()
    part_in[me] = part_out[me]
    stat_in[me] = stat_out[me]

    several(stat_in, n - 1, stat_send, stat_recv).wait_recv()
    got = [stat_in[d] for d in range(n)]
    best = functools.reduce(jnp.maximum, got)
    got = [jnp.exp(g - best) for g in got]
    scale = 1.0 / functools.reduce(jnp.add, got)
    for d in range(n):
        spread[d * own : (d + 1) * own, :] = got[d] * scale
    share = jnp.transpose(spread[...])[:rows]

    several(part_in, n - 1, part_send, part_recv).wait_recv()
    for j in range(own):
        y = jnp.zeros((rows, vdim), jnp.float32)
        for d in range(n):
            at = d * own + j
            y = y + share[:, at : at + 1] * part_in[d, j].astype(jnp.float32)
        flat[me, :, j * vdim : (j + 1) * vdim] = y.astype(jnp.bfloat16)

    flat_copy(mirror, me, 0).start()

    @pl.loop(1, half)
    def _(i):
        flat_copy(near(i), me, 1).start()

    flat_copy(me, mirror, 0).wait_recv()

    @pl.loop(1, half)
    def _(i):
        flat_copy(near(i), mirror, 2).start()

    def multiply(at):
        w_copy(at).wait()
        total = jnp.zeros((rows, w.shape[1]), jnp.float32)
        for t in range(half):
            total = total + lax.dot_general(
                flat[at * half + t],
                w[at, :, t * piece : (t + 1) * piece],
                (((1,), (1,)), ((), ())),
                preferred_element_type=jnp.float32,
            )
        return total

    several(flat, half - 1, flat_send, flat_recv.at[1]).wait_recv()
    total = multiply(side)
    several(flat, half - 1, flat_send, flat_recv.at[2]).wait_recv()
    total = total + multiply(1 - side)
    group[my_head] = total.astype(jnp.bfloat16)

    def group_copy(to, slot):
        return pltpu.make_async_remote_copy(
            src_ref=group.at[slot],
            dst_ref=group.at[slot],
            send_sem=group_send.at[to],
            recv_sem=group_recv.at[slot],
            device_id={"head": to},
            device_id_type=MESH,
        )

    for j in range(1, n_head):
        group_copy(lax.rem(my_head + j, n_head), my_head).start()
    for j in range(1, n_head):
        group_copy(my_head, lax.rem(my_head + j, n_head)).wait_recv()
    out_ref[...] = group[...]

    several(stat_out, n - 1, stat_send, stat_recv).wait_send()
    several(part_out, n - 1, part_send, part_recv).wait_send()
    several(flat, n - 1, flat_send, flat_recv.at[0]).wait_send()
    for j in range(1, n_head):
        group_copy(lax.rem(my_head + j, n_head), my_head).wait_send()


def fused(n, n_head, queries, cache, block_ids, lengths, value_up, out_proj):
    rows, heads, width = queries.shape
    span = cache.shape[1]
    latent, vdim = value_up.shape[1:]
    columns = out_proj.shape[1]
    own = heads // n
    half = n // 2
    dma = pltpu.SemaphoreType.DMA
    any_space = pl.BlockSpec(memory_space=pl.ANY)
    groups = pl.pallas_call(
        functools.partial(kernel, n, n_head),
        out_shape=jax.ShapeDtypeStruct((n_head, rows, columns), jnp.bfloat16),
        in_specs=[
            pl.BlockSpec(memory_space=pltpu.SMEM),
            pl.BlockSpec(memory_space=pltpu.VMEM),
            any_space,
            any_space,
            any_space,
            any_space,
        ],
        out_specs=pl.BlockSpec(memory_space=pltpu.VMEM),
        scratch_shapes=[
            pltpu.VMEM((rows, heads, width), jnp.bfloat16),
            pltpu.VMEM((rows, width, span), jnp.bfloat16),
            pltpu.VMEM((heads, latent, vdim), jnp.bfloat16),
            pltpu.VMEM((2, columns, half * own * vdim), jnp.bfloat16),
            pltpu.VMEM((rows, heads // 2, span), jnp.float32),
            pltpu.VMEM((latent // 128, rows * heads // 2, 128), jnp.float32),
            pltpu.VMEM((n, own, 128), jnp.float32),
            pltpu.VMEM((n, own, 128), jnp.float32),
            pltpu.VMEM((heads, 128), jnp.float32),
            pltpu.VMEM((n, own, rows, vdim), jnp.bfloat16),
            pltpu.VMEM((n, own, rows, vdim), jnp.bfloat16),
            pltpu.VMEM((n, rows, own * vdim), jnp.bfloat16),
            pltpu.VMEM((n_head, rows, columns), jnp.bfloat16),
            dma((2, GROUPS)),
            dma((half,)),
            dma((2,)),
            dma,
            dma,
            dma,
            dma,
            dma,
            dma((3,)),
            dma((n_head,)),
            dma((n_head,)),
        ],
        compiler_params=pltpu.CompilerParams(
            collective_id=0, has_side_effects=True, vmem_limit_bytes=60 * 2**20
        ),
    )(
        lengths,
        block_ids,
        queries,
        jnp.transpose(cache, (0, 2, 1)),
        value_up,
        jnp.transpose(out_proj),
    )
    return jnp.sum(groups.astype(jnp.float32), axis=0).astype(jnp.bfloat16)


def spread_body(queries, cache, block_ids, lengths, value_up, out_proj):
    rows, span, width = cache.shape
    latent = value_up.shape[1]
    first = lax.axis_index("seq") * span
    position = first + jnp.arange(span, dtype=jnp.int32)
    chosen = jnp.any(block_ids[:, :, None] == (position // BLOCK)[None, None, :], axis=1)
    live = chosen & (position[None, :] < lengths[:, None])
    scores = (
        jnp.einsum("rhc,rsc->rhs", queries, cache, preferred_element_type=jnp.float32)
        * softmax_scale
    )
    masked = jnp.where(live[:, None, :], scores, -jnp.inf)
    local_top = jnp.max(masked, axis=-1)
    top = lax.pmax(local_top, "seq")
    expo = jnp.where(live[:, None, :], jnp.exp(masked - top[:, :, None]), jnp.float32(0.0))
    local_total = jnp.sum(expo, axis=-1)
    weights = expo.astype(jnp.bfloat16)
    summed = jnp.einsum(
        "rhs,rsc->rhc", weights, cache[:, :, :latent], preferred_element_type=jnp.float32
    )
    upward = value_up.astype(jnp.float32)
    total, summed_all = lax.psum((local_total, summed), "seq")
    context = summed_all / total[:, :, None]
    heads_out = jnp.einsum("rhc,hcv->rhv", context, upward, precision=lax.Precision.HIGHEST)
    flat = heads_out.astype(jnp.bfloat16).reshape(rows, -1)
    partial_out = jnp.dot(flat, out_proj, preferred_element_type=jnp.float32)
    return lax.psum(partial_out.astype(jnp.bfloat16), "head")


def body(n, n_head, *args):
    heads, span = args[0].shape[1], args[1].shape[1]
    if heads % n or n % 4 or span % BLOCK or span % 128:
        return spread_body(*args)
    return fused(n, n_head, *args)


def solution(mesh):
    return jax.shard_map(
        functools.partial(body, mesh.shape["seq"], mesh.shape["head"]),
        mesh=mesh,
        in_specs=(
            P(None, "head", None),
            P(None, "seq", None),
            P(),
            P(),
            P("head", None, None),
            P("head", "seq"),
        ),
        out_specs=P(None, "seq"),
        check_vma=False,
    )
```

time: 30.5 us -> 28.7 us (0.941)
  Pallas kernels: 28.8 us -> 27.1 us
  other arithmetic: 0 us -> 1.38 us
  local copies, waits for them, and re-layouts: 1.32 us -> 0 us
    pallas_call x1, Pallas kernels: 28.8 us -> 27.1 us  [fused(): pl.pallas_call(functools.partial(kernel, n, n_head), out_shape=jax.ShapeD...]
    reduce_sum x0 -> x1, other arithmetic: none -> 1.38 us  [fused(): return jnp.sum(groups.astype(jnp.float32), axis=0).astype(jnp.bfloat16)]
    unnamed x1 -> x0, local copies, waits for them, and re-layouts: 1.32 us -> none
where the time goes in v3:
time: 28.7 us; the launch traced here: 28.4 us
  Pallas kernels  27.1 us (94%)
  other arithmetic  1.38 us (5%)
    pallas_call x1, Pallas kernels, fused(): pl.pallas_call(functools.partial(kernel, n, n_head), out_shape=jax.ShapeD...  27.1 us
    reduce_sum x1, other arithmetic, fused(): return jnp.sum(groups.astype(jnp.float32), axis=0).astype(jnp.bfloat16)  1.38 us

profile of v3, /device:TPU:0, one launch (start us, length us, event | category | flops | bytes accessed | tf_op | source)
XLA Modules:
  0.0 28.4 jit_solution(17858448403830644976)
XLA Ops:
  0.0 27.1 %shard_map.64 = bf16[2,16,448]{2,1,0:T(8,128)(2,1)} custom-call(s32[16]{0:T(128)} %lengths_ref.1, s32[16,32]{1,0:T(8,128)} %ids_ref.1, bf16[16,64,576]{2,1,0:T(8,128)(2,1)} %q_hbm.1, bf16[16,576,128]{2,1,0:T(8,128)(2,1)} %bitcast.3, bf16[64,512,128]{2,1,0:T(8,128)(2,1)} %v_hbm.1, bf16[448,8192]{1,0:T(8,128)(2,1)} %bitcast.2), custom_call_target="tpu_custom_call" | custom-call | tf_op jit(solution)/shard_map/pallas_call | solution.py:323
  27.1 1.4 %reduce_sum.12 = bf16[16,448]{1,0:T(8,128)(2,1)} reduce(bf16[2,16,448]{2,1,0:T(8,128)(2,1)} %shard_map.64, bf16[]{:T(256)} %constant.2.clone.1), dimensions={0}, to_apply=%region_0.0 | reduce | flops 7168 | bytes 43010 | tf_op jit(solution)/shard_map/reduce_sum | solution.py:372

commit v4 on v3

--- a/solution.py
+++ b/solution.py
@@ -10,6 +10,7 @@
 BLOCK = 64
 DEAD = -1e30
 GROUPS = 4
+BATCH = 8
 MESH = pl.DeviceIdType.MESH
 
 
@@ -19,13 +20,15 @@
 def kernel(
     n,
     n_head,
-    lengths_ref,
-    ids_ref,
+    lengths_hbm,
+    ids_hbm,
     q_hbm,
     k_hbm,
     v_hbm,
     w_hbm,
     out_ref,
+    lengths_ref,
+    ids_ref,
     q,
     k,
     v,
@@ -39,6 +42,7 @@
     part_in,
     flat,
     group,
+    small_sem,
     local_sem,
     v_sem,
     w_sem,
@@ -87,6 +91,12 @@
     def pair_at(other, i):
         return other * pairs + lax.rem(place // 2 + 1 + i, pairs)
 
+    small_copies = (
+        pltpu.make_async_copy(ids_hbm, ids_ref, small_sem.at[0]),
+        pltpu.make_async_copy(lengths_hbm, lengths_ref, small_sem.at[1]),
+    )
+    for copy in small_copies:
+        copy.start()
     for g in range(GROUPS):
         for copy in first_copies(g):
             copy.start()
@@ -104,6 +114,8 @@
             barrier, inc=1, device_id={"head": lax.rem(my_head + j, n_head)}, device_id_type=MESH
         )
 
+    for copy in small_copies:
+        copy.wait()
     lane = lax.broadcasted_iota(jnp.int32, (rows, span), 1)
     line = lax.broadcasted_iota(jnp.int32, (rows, span), 0)
     first = me * span
@@ -177,40 +189,52 @@
             w_copy(1 - side).start()
         stats = jnp.zeros((some_heads, 128), jnp.float32)
         stat_lane = lax.broadcasted_iota(jnp.int32, (some_heads, 128), 1)
-        for r in range(rows):
-            s = scores[r]
-            top = jnp.max(s, axis=1, keepdims=True)
-            expo = jnp.where(live[r : r + 1] > 0.0, jnp.exp(s - top), 0.0)
-            total = jnp.sum(expo, axis=1, keepdims=True)
+        for r0 in range(0, rows, BATCH):
+            s = scores[r0 : r0 + BATCH]
+            top = jnp.max(s, axis=2, keepdims=True)
+            expo = jnp.where(s > 0.5 * DEAD, jnp.exp(s - top), 0.0)
+            total = jnp.sum(expo, axis=2, keepdims=True)
             some = total > 0.0
             total = jnp.where(some, total, 1.0)
-            stats = jnp.where(stat_lane == r, jnp.where(some, top + jnp.log(total), DEAD), stats)
-            out = lax.dot_general(
-                expo.astype(jnp.bfloat16),
-                k[r, :latent, :],
-                (((1,), (1,)), ((), ())),
-                preferred_element_type=jnp.float32,
-            )
-            out = out * (1.0 / total)
-            for c in range(tiles):
-                summed[c, r * some_heads : (r + 1) * some_heads, :] = out[
-                    :, c * 128 : (c + 1) * 128
-                ]
+            log_sum = jnp.where(some, top + jnp.log(total), DEAD)
+            inverse = 1.0 / total
+            weights = expo.astype(jnp.bfloat16)
+            for i in range(BATCH):
+                r = r0 + i
+                stats = jnp.where(stat_lane == r, log_sum[i], stats)
+                out = lax.dot_general(
+                    weights[i],
+                    k[r, :latent, :],
+                    (((1,), (1,)), ((), ())),
+                    preferred_element_type=jnp.float32,
+                )
+                out = out * inverse[i]
+                for c in range(tiles):
+                    summed[c, r * some_heads : (r + 1) * some_heads, :] = out[
+                        :, c * 128 : (c + 1) * 128
+                    ]
         for t in range(half):
             stat_out[other * half + t] = stats[t * own : (t + 1) * own]
 
     def project(other, pair):
         v_copy(pair).wait()
-        for j in range(2 * own):
-            h = pair * (2 * own) + j
-            x = jnp.concatenate(
+        first_head = pair * (2 * own)
+        local_head = first_head - other * some_heads
+        contexts = [
+            jnp.concatenate(
                 [
-                    summed[c, pl.ds(h - other * some_heads, rows, stride=some_heads), :]
+                    summed[c, pl.ds(local_head + j, rows, stride=some_heads), :]
                     for c in range(tiles)
                 ],
                 axis=1,
-            )
-            y = jnp.dot(x.astype(jnp.bfloat16), v[h], preferred_element_type=jnp.float32)
+            ).astype(jnp.bfloat16)
+            for j in range(2 * own)
+        ]
+        parts = [
+            jnp.dot(x, v[first_head + j], preferred_element_type=jnp.float32)
+            for j, x in enumerate(contexts)
+        ]
+        for j, y in enumerate(parts):
             part_out[2 * pair + j // own, j % own] = y.astype(jnp.bfloat16)
 
     attend(1 - side, True)
@@ -319,20 +343,15 @@
     own = heads // n
     half = n // 2
     dma = pltpu.SemaphoreType.DMA
-    any_space = pl.BlockSpec(memory_space=pl.ANY)
+    in_hbm = pl.BlockSpec(memory_space=pltpu.HBM)
     groups = pl.pallas_call(
         functools.partial(kernel, n, n_head),
         out_shape=jax.ShapeDtypeStruct((n_head, rows, columns), jnp.bfloat16),
-        in_specs=[
-            pl.BlockSpec(memory_space=pltpu.SMEM),
-            pl.BlockSpec(memory_space=pltpu.VMEM),
-            any_space,
-            any_space,
-            any_space,
-            any_space,
-        ],
+        in_specs=[in_hbm] * 6,
         out_specs=pl.BlockSpec(memory_space=pltpu.VMEM),
         scratch_shapes=[
+            pltpu.SMEM(lengths.shape, jnp.int32),
+            pltpu.VMEM(block_ids.shape, jnp.int32),
             pltpu.VMEM((rows, heads, width), jnp.bfloat16),
             pltpu.VMEM((rows, width, span), jnp.bfloat16),
             pltpu.VMEM((heads, latent, vdim), jnp.bfloat16),
@@ -346,6 +365,7 @@
             pltpu.VMEM((n, own, rows, vdim), jnp.bfloat16),
             pltpu.VMEM((n, rows, own * vdim), jnp.bfloat16),
             pltpu.VMEM((n_head, rows, columns), jnp.bfloat16),
+            dma((2,)),
             dma((2, GROUPS)),
             dma((half,)),
             dma((2,)),

time: 28.7 us -> 28 us (0.976)
  Pallas kernels: 27.1 us -> 26.4 us
    pallas_call x1, Pallas kernels: 27.1 us -> 26.4 us  [fused(): pl.pallas_call(functools.partial(kernel, n, n_head), out_shape=jax.ShapeD...]
where the time goes in v4:
time: 28 us; the launch traced here: 27.8 us
  Pallas kernels  26.4 us (94%)
  other arithmetic  1.38 us (5%)
    pallas_call x1, Pallas kernels, fused(): pl.pallas_call(functools.partial(kernel, n, n_head), out_shape=jax.ShapeD...  26.4 us
    reduce_sum x1, other arithmetic, fused(): return jnp.sum(groups.astype(jnp.float32), axis=0).astype(jnp.bfloat16)  1.38 us

profile of v4, /device:TPU:0, one launch (start us, length us, event | category | flops | bytes accessed | tf_op | source)
XLA Modules:
  0.0 27.8 jit_solution(7808693696582012944)
XLA Ops:
  0.0 26.4 %shard_map.64 = bf16[2,16,448]{2,1,0:T(8,128)(2,1)} custom-call(s32[16]{0:T(128)} %lengths_hbm.1, s32[16,32]{1,0:T(8,128)} %ids_hbm.1, bf16[16,64,576]{2,1,0:T(8,128)(2,1)} %q_hbm.1, bf16[16,576,128]{2,1,0:T(8,128)(2,1)} %bitcast.3, bf16[64,512,128]{2,1,0:T(8,128)(2,1)} %v_hbm.1, bf16[448,8192]{1,0:T(8,128)(2,1)} %bitcast.2), custom_call_target="tpu_custom_call" | custom-call | tf_op jit(solution)/shard_map/pallas_call | solution.py:347
  26.4 1.4 %reduce_sum.12 = bf16[16,448]{1,0:T(8,128)(2,1)} reduce(bf16[2,16,448]{2,1,0:T(8,128)(2,1)} %shard_map.64, bf16[]{:T(256)} %constant.2.clone.1), dimensions={0}, to_apply=%region_0.0 | reduce | flops 7168 | bytes 43010 | tf_op jit(solution)/shard_map/reduce_sum | solution.py:392

commit v5 on v4

--- a/solution.py
+++ b/solution.py
@@ -64,7 +64,6 @@
     me = lax.axis_index("seq")
     my_head = lax.axis_index("head")
     half = n // 2
-    pairs = half // 2
     some_heads = heads // 2
     side = me // half
     place = lax.rem(me, half)
@@ -80,16 +79,13 @@
             pltpu.make_async_copy(k_hbm.at[part], k.at[part], local_sem.at[1, g]),
         )
 
-    def v_copy(pair):
-        part = pl.ds(pair * (2 * own), 2 * own)
-        return pltpu.make_async_copy(v_hbm.at[part], v.at[part], v_sem.at[pair])
+    def v_copy(at):
+        part = pl.ds(at * some_heads, some_heads)
+        return pltpu.make_async_copy(v_hbm.at[part], v.at[part], v_sem.at[at])
 
     def w_copy(at):
         part = pl.ds(pl.multiple_of(at * (half * piece), half * piece), half * piece)
         return pltpu.make_async_copy(w_hbm.at[:, part], w.at[at], w_sem.at[at])
-
-    def pair_at(other, i):
-        return other * pairs + lax.rem(place // 2 + 1 + i, pairs)
 
     small_copies = (
         pltpu.make_async_copy(ids_hbm, ids_ref, small_sem.at[0]),
@@ -181,10 +177,8 @@
             )
             scores[r] = jnp.where(live[r : r + 1] > 0.0, s * softmax_scale, DEAD)
         if opening:
-            for i in range(pairs):
-                v_copy(pair_at(other, i)).start()
-            for i in range(pairs):
-                v_copy(pair_at(1 - other, i)).start()
+            v_copy(other).start()
+            v_copy(1 - other).start()
             w_copy(side).start()
             w_copy(1 - side).start()
         stats = jnp.zeros((some_heads, 128), jnp.float32)
@@ -216,52 +210,42 @@
         for t in range(half):
             stat_out[other * half + t] = stats[t * own : (t + 1) * own]
 
-    def project(other, pair):
-        v_copy(pair).wait()
-        first_head = pair * (2 * own)
-        local_head = first_head - other * some_heads
-        contexts = [
-            jnp.concatenate(
-                [
-                    summed[c, pl.ds(local_head + j, rows, stride=some_heads), :]
-                    for c in range(tiles)
-                ],
-                axis=1,
-            ).astype(jnp.bfloat16)
-            for j in range(2 * own)
-        ]
-        parts = [
-            jnp.dot(x, v[first_head + j], preferred_element_type=jnp.float32)
-            for j, x in enumerate(contexts)
-        ]
-        for j, y in enumerate(parts):
-            part_out[2 * pair + j // own, j % own] = y.astype(jnp.bfloat16)
+    def project(other):
+        v_copy(other).wait()
+        for j0 in range(0, some_heads, 2 * own):
+            contexts = [
+                jnp.concatenate(
+                    [summed[c, pl.ds(j, rows, stride=some_heads), :] for c in range(tiles)],
+                    axis=1,
+                ).astype(jnp.bfloat16)
+                for j in range(j0, j0 + 2 * own)
+            ]
+            parts = [
+                jnp.dot(x, v[other * some_heads + j0 + j], preferred_element_type=jnp.float32)
+                for j, x in enumerate(contexts)
+            ]
+            for j, y in enumerate(parts):
+                h = j0 + j
+                part_out[other * half + h // own, h % own] = y.astype(jnp.bfloat16)
 
     attend(1 - side, True)
+    project(1 - side)
     pl.semaphore_wait(barrier, n - 1 + n_head - 1)
 
-    @pl.loop(0, pairs)
+    @pl.loop(0, half)
     def _(i):
-        pair = pair_at(1 - side, i)
-        project(1 - side, pair)
-        for t in (2 * pair, 2 * pair + 1):
-            part_copy(t).start()
-            stat_copy(t).start()
+        t = (1 - side) * half + lax.rem(place + i, half)
+        part_copy(t).start()
+        stat_copy(t).start()
 
     attend(side, False)
-
-    @pl.loop(0, pairs - 1)
+    project(side)
+
+    @pl.loop(1, half)
     def _(i):
-        pair = pair_at(side, i)
-        project(side, pair)
-        for t in (2 * pair, 2 * pair + 1):
-            part_copy(t).start()
-            stat_copy(t).start()
-
-    project(side, me // 2)
-    beside = me // 2 * 2 + 1 - lax.rem(me, 2)
-    part_copy(beside).start()
-    stat_copy(beside).start()
+        part_copy(near(i)).start()
+        stat_copy(near(i)).start()
+
     part_in[me] = part_out[me]
     stat_in[me] = stat_out[me]
 
@@ -367,7 +351,7 @@
             pltpu.VMEM((n_head, rows, columns), jnp.bfloat16),
             dma((2,)),
             dma((2, GROUPS)),
-            dma((half,)),
+            dma((2,)),
             dma((2,)),
             dma,
             dma,

time: 28 us -> 29 us (1.036)
  Pallas kernels: 26.4 us -> 27.4 us
    pallas_call x1, Pallas kernels: 26.4 us -> 27.4 us  [fused(): pl.pallas_call(functools.partial(kernel, n, n_head), out_shape=jax.ShapeD...]
where the time goes in v5:
time: 29 us; the launch traced here: 28.8 us
  Pallas kernels  27.4 us (94%)
  other arithmetic  1.38 us (5%)
    pallas_call x1, Pallas kernels, fused(): pl.pallas_call(functools.partial(kernel, n, n_head), out_shape=jax.ShapeD...  27.4 us
    reduce_sum x1, other arithmetic, fused(): return jnp.sum(groups.astype(jnp.float32), axis=0).astype(jnp.bfloat16)  1.38 us

profile of v5, /device:TPU:0, one launch (start us, length us, event | category | flops | bytes accessed | tf_op | source)
XLA Modules:
  0.0 28.8 jit_solution(14006444571540901324)
XLA Ops:
  0.0 27.4 %shard_map.64 = bf16[2,16,448]{2,1,0:T(8,128)(2,1)} custom-call(s32[16]{0:T(128)} %lengths_hbm.1, s32[16,32]{1,0:T(8,128)} %ids_hbm.1, bf16[16,64,576]{2,1,0:T(8,128)(2,1)} %q_hbm.1, bf16[16,576,128]{2,1,0:T(8,128)(2,1)} %bitcast.3, bf16[64,512,128]{2,1,0:T(8,128)(2,1)} %v_hbm.1, bf16[448,8192]{1,0:T(8,128)(2,1)} %bitcast.2), custom_call_target="tpu_custom_call" | custom-call | tf_op jit(solution)/shard_map/pallas_call | solution.py:331
  27.4 1.4 %reduce_sum.12 = bf16[16,448]{1,0:T(8,128)(2,1)} reduce(bf16[2,16,448]{2,1,0:T(8,128)(2,1)} %shard_map.64, bf16[]{:T(256)} %constant.2.clone.1), dimensions={0}, to_apply=%region_0.0 | reduce | flops 7168 | bytes 43010 | tf_op jit(solution)/shard_map/reduce_sum | solution.py:376

commit v6 on v4

--- a/solution.py
+++ b/solution.py
@@ -174,19 +174,19 @@
         at = pl.multiple_of(other * some_heads, some_heads)
         for r in range(rows):
             if opening and r % (rows // GROUPS) == 0:
-                for copy in first_copies(r // (rows // GROUPS)):
+                g = r // (rows // GROUPS)
+                for copy in first_copies(g):
                     copy.wait()
+                if g == 0:
+                    for i in range(pairs):
+                        v_copy(pair_at(other, i)).start()
+                if g == GROUPS - 1:
+                    for i in range(pairs):
+                        v_copy(pair_at(1 - other, i)).start()
             s = jnp.dot(
                 q[r, pl.ds(at, some_heads), :], k[r], preferred_element_type=jnp.float32
             )
             scores[r] = jnp.where(live[r : r + 1] > 0.0, s * softmax_scale, DEAD)
-        if opening:
-            for i in range(pairs):
-                v_copy(pair_at(other, i)).start()
-            for i in range(pairs):
-                v_copy(pair_at(1 - other, i)).start()
-            w_copy(side).start()
-            w_copy(1 - side).start()
         stats = jnp.zeros((some_heads, 128), jnp.float32)
         stat_lane = lax.broadcasted_iota(jnp.int32, (some_heads, 128), 1)
         for r0 in range(0, rows, BATCH):
@@ -248,6 +248,8 @@
             part_copy(t).start()
             stat_copy(t).start()
 
+    w_copy(side).start()
+    w_copy(1 - side).start()
     attend(side, False)
 
     @pl.loop(0, pairs - 1)

time: 28 us -> 27.1 us (0.968)
  Pallas kernels: 26.4 us -> 25.5 us
    pallas_call x1, Pallas kernels: 26.4 us -> 25.5 us  [fused(): pl.pallas_call(functools.partial(kernel, n, n_head), out_shape=jax.ShapeD...]
where the time goes in v6:
time: 27.1 us; the launch traced here: 26.9 us
  Pallas kernels  25.5 us (94%)
  other arithmetic  1.38 us (5%)
    pallas_call x1, Pallas kernels, fused(): pl.pallas_call(functools.partial(kernel, n, n_head), out_shape=jax.ShapeD...  25.5 us
    reduce_sum x1, other arithmetic, fused(): return jnp.sum(groups.astype(jnp.float32), axis=0).astype(jnp.bfloat16)  1.38 us

profile of v6, /device:TPU:0, one launch (start us, length us, event | category | flops | bytes accessed | tf_op | source)
XLA Modules:
  0.0 26.9 jit_solution(9729578308284052822)
XLA Ops:
  0.0 25.5 %shard_map.64 = bf16[2,16,448]{2,1,0:T(8,128)(2,1)} custom-call(s32[16]{0:T(128)} %lengths_hbm.1, s32[16,32]{1,0:T(8,128)} %ids_hbm.1, bf16[16,64,576]{2,1,0:T(8,128)(2,1)} %q_hbm.1, bf16[16,576,128]{2,1,0:T(8,128)(2,1)} %bitcast.3, bf16[64,512,128]{2,1,0:T(8,128)(2,1)} %v_hbm.1, bf16[448,8192]{1,0:T(8,128)(2,1)} %bitcast.2), custom_call_target="tpu_custom_call" | custom-call | tf_op jit(solution)/shard_map/pallas_call | solution.py:349
  25.5 1.4 %reduce_sum.12 = bf16[16,448]{1,0:T(8,128)(2,1)} reduce(bf16[2,16,448]{2,1,0:T(8,128)(2,1)} %shard_map.64, bf16[]{:T(256)} %constant.2.clone.1), dimensions={0}, to_apply=%region_0.0 | reduce | flops 7168 | bytes 43010 | tf_op jit(solution)/shard_map/reduce_sum | solution.py:394

commit v7 on v6

--- a/solution.py
+++ b/solution.py
@@ -75,10 +75,18 @@
 
     def first_copies(g):
         part = pl.ds(g * (rows // GROUPS), rows // GROUPS)
+        far = half_heads(1 - side)
         return (
-            pltpu.make_async_copy(q_hbm.at[part], q.at[part], local_sem.at[0, g]),
+            pltpu.make_async_copy(q_hbm.at[part, far], q.at[part, far], local_sem.at[0, g]),
             pltpu.make_async_copy(k_hbm.at[part], k.at[part], local_sem.at[1, g]),
         )
+
+    def half_heads(other):
+        return pl.ds(pl.multiple_of(other * some_heads, some_heads), some_heads)
+
+    def near_queries():
+        part = half_heads(side)
+        return pltpu.make_async_copy(q_hbm.at[:, part], q.at[:, part], small_sem.at[2])
 
     def v_copy(pair):
         part = pl.ds(pair * (2 * own), 2 * own)
@@ -171,7 +179,6 @@
         )
 
     def attend(other, opening):
-        at = pl.multiple_of(other * some_heads, some_heads)
         for r in range(rows):
             if opening and r % (rows // GROUPS) == 0:
                 g = r // (rows // GROUPS)
@@ -181,10 +188,11 @@
                     for i in range(pairs):
                         v_copy(pair_at(other, i)).start()
                 if g == GROUPS - 1:
+                    near_queries().start()
                     for i in range(pairs):
                         v_copy(pair_at(1 - other, i)).start()
             s = jnp.dot(
-                q[r, pl.ds(at, some_heads), :], k[r], preferred_element_type=jnp.float32
+                q[r, half_heads(other), :], k[r], preferred_element_type=jnp.float32
             )
             scores[r] = jnp.where(live[r : r + 1] > 0.0, s * softmax_scale, DEAD)
         stats = jnp.zeros((some_heads, 128), jnp.float32)
@@ -216,9 +224,7 @@
         for t in range(half):
             stat_out[other * half + t] = stats[t * own : (t + 1) * own]
 
-    def project(other, pair):
-        v_copy(pair).wait()
-        first_head = pair * (2 * own)
+    def project(other, first_head, count):
         local_head = first_head - other * some_heads
         contexts = [
             jnp.concatenate(
@@ -228,14 +234,14 @@
                 ],
                 axis=1,
             ).astype(jnp.bfloat16)
-            for j in range(2 * own)
+            for j in range(count)
         ]
         parts = [
             jnp.dot(x, v[first_head + j], preferred_element_type=jnp.float32)
             for j, x in enumerate(contexts)
         ]
         for j, y in enumerate(parts):
-            part_out[2 * pair + j // own, j % own] = y.astype(jnp.bfloat16)
+            part_out[first_head // own + j // own, j % own] = y.astype(jnp.bfloat16)
 
     attend(1 - side, True)
     pl.semaphore_wait(barrier, n - 1 + n_head - 1)
@@ -243,27 +249,32 @@
     @pl.loop(0, pairs)
     def _(i):
         pair = pair_at(1 - side, i)
-        project(1 - side, pair)
+        v_copy(pair).wait()
+        project(1 - side, 2 * pair * own, 2 * own)
         for t in (2 * pair, 2 * pair + 1):
             part_copy(t).start()
             stat_copy(t).start()
 
     w_copy(side).start()
     w_copy(1 - side).start()
+    near_queries().wait()
     attend(side, False)
 
     @pl.loop(0, pairs - 1)
     def _(i):
         pair = pair_at(side, i)
-        project(side, pair)
+        v_copy(pair).wait()
+        project(side, 2 * pair * own, 2 * own)
         for t in (2 * pair, 2 * pair + 1):
             part_copy(t).start()
             stat_copy(t).start()
 
-    project(side, me // 2)
     beside = me // 2 * 2 + 1 - lax.rem(me, 2)
+    v_copy(me // 2).wait()
+    project(side, beside * own, own)
     part_copy(beside).start()
     stat_copy(beside).start()
+    project(side, me * own, own)
     part_in[me] = part_out[me]
     stat_in[me] = stat_out[me]
 
@@ -312,12 +323,12 @@
     total = multiply(side)
     several(flat, half - 1, flat_send, flat_recv.at[2]).wait_recv()
     total = total + multiply(1 - side)
-    group[my_head] = total.astype(jnp.bfloat16)
+    group[...] = total.astype(jnp.bfloat16)
 
     def group_copy(to, slot):
         return pltpu.make_async_remote_copy(
-            src_ref=group.at[slot],
-            dst_ref=group.at[slot],
+            src_ref=group,
+            dst_ref=out_ref.at[slot],
             send_sem=group_send.at[to],
             recv_sem=group_recv.at[slot],
             device_id={"head": to},
@@ -326,15 +337,17 @@
 
     for j in range(1, n_head):
         group_copy(lax.rem(my_head + j, n_head), my_head).start()
-    for j in range(1, n_head):
-        group_copy(my_head, lax.rem(my_head + j, n_head)).wait_recv()
-    out_ref[...] = group[...]
+    own_group = pltpu.make_async_copy(group, out_ref.at[my_head], group_recv.at[my_head])
+    own_group.start()
 
     several(stat_out, n - 1, stat_send, stat_recv).wait_send()
     several(part_out, n - 1, part_send, part_recv).wait_send()
     several(flat, n - 1, flat_send, flat_recv.at[0]).wait_send()
     for j in range(1, n_head):
         group_copy(lax.rem(my_head + j, n_head), my_head).wait_send()
+    own_group.wait()
+    for j in range(1, n_head):
+        group_copy(my_head, lax.rem(my_head + j, n_head)).wait_recv()
 
 
 def fused(n, n_head, queries, cache, block_ids, lengths, value_up, out_proj):
@@ -350,7 +363,7 @@
         functools.partial(kernel, n, n_head),
         out_shape=jax.ShapeDtypeStruct((n_head, rows, columns), jnp.bfloat16),
         in_specs=[in_hbm] * 6,
-        out_specs=pl.BlockSpec(memory_space=pltpu.VMEM),
+        out_specs=in_hbm,
         scratch_shapes=[
             pltpu.SMEM(lengths.shape, jnp.int32),
             pltpu.VMEM(block_ids.shape, jnp.int32),
@@ -366,8 +379,8 @@
             pltpu.VMEM((n, own, rows, vdim), jnp.bfloat16),
             pltpu.VMEM((n, own, rows, vdim), jnp.bfloat16),
             pltpu.VMEM((n, rows, own * vdim), jnp.bfloat16),
-            pltpu.VMEM((n_head, rows, columns), jnp.bfloat16),
-            dma((2,)),
+            pltpu.VMEM((rows, columns), jnp.bfloat16),
+            dma((3,)),
             dma((2, GROUPS)),
             dma((half,)),
             dma((2,)),

time: 27.1 us -> 26.6 us (0.982)
  Pallas kernels: 25.5 us -> 25 us
    pallas_call x1, Pallas kernels: 25.5 us -> 25 us  [fused(): pl.pallas_call(functools.partial(kernel, n, n_head), out_shape=jax.ShapeD...]
where the time goes in v7:
time: 26.6 us; the launch traced here: 26.4 us
  Pallas kernels  25 us (94%)
  other arithmetic  1.38 us (5%)
    pallas_call x1, Pallas kernels, fused(): pl.pallas_call(functools.partial(kernel, n, n_head), out_shape=jax.ShapeD...  25 us
    reduce_sum x1, other arithmetic, fused(): return jnp.sum(groups.astype(jnp.float32), axis=0).astype(jnp.bfloat16)  1.38 us

profile of v7, /device:TPU:0, one launch (start us, length us, event | category | flops | bytes accessed | tf_op | source)
XLA Modules:
  0.0 26.4 jit_solution(7680660278478861693)
XLA Ops:
  0.0 25.0 %shard_map.64 = bf16[2,16,448]{2,1,0:T(8,128)(2,1)} custom-call(s32[16]{0:T(128)} %lengths_hbm.1, s32[16,32]{1,0:T(8,128)} %ids_hbm.1, bf16[16,64,576]{2,1,0:T(8,128)(2,1)} %q_hbm.1, bf16[16,576,128]{2,1,0:T(8,128)(2,1)} %bitcast.3, bf16[64,512,128]{2,1,0:T(8,128)(2,1)} %v_hbm.1, bf16[448,8192]{1,0:T(8,128)(2,1)} %bitcast.2), custom_call_target="tpu_custom_call" | custom-call | tf_op jit(solution)/shard_map/pallas_call | solution.py:362
  25.0 1.4 %reduce_sum.12 = bf16[16,448]{1,0:T(8,128)(2,1)} reduce(bf16[2,16,448]{2,1,0:T(8,128)(2,1)} %shard_map.64, bf16[]{:T(256)} %constant.2.clone.1), dimensions={0}, to_apply=%region_0.0 | reduce | flops 7168 | bytes 43010 | tf_op jit(solution)/shard_map/reduce_sum | solution.py:407

commit v8 on v7

--- a/solution.py
+++ b/solution.py
@@ -305,24 +305,31 @@
 
     @pl.loop(1, half)
     def _(i):
-        flat_copy(near(i), mirror, 2).start()
-
-    def multiply(at):
-        w_copy(at).wait()
-        total = jnp.zeros((rows, w.shape[1]), jnp.float32)
-        for t in range(half):
-            total = total + lax.dot_general(
-                flat[at * half + t],
-                w[at, :, t * piece : (t + 1) * piece],
-                (((1,), (1,)), ((), ())),
-                preferred_element_type=jnp.float32,
-            )
-        return total
+        flat_copy(near(i), mirror, 2 + place).start()
+
+    def multiply(at, t):
+        part = t * piece if isinstance(t, int) else pl.multiple_of(t * piece, piece)
+        return lax.dot_general(
+            flat[at * half + t],
+            w[at, :, pl.ds(part, piece)],
+            (((1,), (1,)), ((), ())),
+            preferred_element_type=jnp.float32,
+        )
 
     several(flat, half - 1, flat_send, flat_recv.at[1]).wait_recv()
-    total = multiply(side)
-    several(flat, half - 1, flat_send, flat_recv.at[2]).wait_recv()
-    total = total + multiply(1 - side)
+    w_copy(side).wait()
+    w_copy(1 - side).wait()
+    total = multiply(side, 0)
+    for t in range(1, half):
+        total = total + multiply(side, t)
+    total = total + multiply(1 - side, place)
+
+    def arrived(i, total):
+        t = lax.rem(place + half - i, half)
+        flat_copy(me, (1 - side) * half + t, 2 + t).wait_recv()
+        return total + multiply(1 - side, t)
+
+    total = lax.fori_loop(1, half, arrived, total)
     group[...] = total.astype(jnp.bfloat16)
 
     def group_copy(to, slot):
@@ -389,7 +396,7 @@
             dma,
             dma,
             dma,
-            dma((3,)),
+            dma((2 + half,)),
             dma((n_head,)),
             dma((n_head,)),
         ],

time: 26.6 us -> 27.2 us (1.023)
  Pallas kernels: 25 us -> 25.7 us
    pallas_call x1, Pallas kernels: 25 us -> 25.7 us  [fused(): pl.pallas_call(functools.partial(kernel, n, n_head), out_shape=jax.ShapeD...]
where the time goes in v8:
time: 27.2 us; the launch traced here: 27 us
  Pallas kernels  25.7 us (94%)
  other arithmetic  1.38 us (5%)
    pallas_call x1, Pallas kernels, fused(): pl.pallas_call(functools.partial(kernel, n, n_head), out_shape=jax.ShapeD...  25.7 us
    reduce_sum x1, other arithmetic, fused(): return jnp.sum(groups.astype(jnp.float32), axis=0).astype(jnp.bfloat16)  1.38 us

profile of v8, /device:TPU:0, one launch (start us, length us, event | category | flops | bytes accessed | tf_op | source)
XLA Modules:
  0.0 27.0 jit_solution(14961605239046485465)
XLA Ops:
  0.0 25.7 %shard_map.64 = bf16[2,16,448]{2,1,0:T(8,128)(2,1)} custom-call(s32[16]{0:T(128)} %lengths_hbm.1, s32[16,32]{1,0:T(8,128)} %ids_hbm.1, bf16[16,64,576]{2,1,0:T(8,128)(2,1)} %q_hbm.1, bf16[16,576,128]{2,1,0:T(8,128)(2,1)} %bitcast.3, bf16[64,512,128]{2,1,0:T(8,128)(2,1)} %v_hbm.1, bf16[448,8192]{1,0:T(8,128)(2,1)} %bitcast.2), custom_call_target="tpu_custom_call" | custom-call | tf_op jit(solution)/shard_map/pallas_call | solution.py:369
  25.7 1.4 %reduce_sum.12 = bf16[16,448]{1,0:T(8,128)(2,1)} reduce(bf16[2,16,448]{2,1,0:T(8,128)(2,1)} %shard_map.64, bf16[]{:T(256)} %constant.2.clone.1), dimensions={0}, to_apply=%region_0.0 | reduce | flops 7168 | bytes 43010 | tf_op jit(solution)/shard_map/reduce_sum | solution.py:414

commit v9 on v7

--- a/solution.py
+++ b/solution.py
@@ -38,6 +38,7 @@
     stat_out,
     stat_in,
     spread,
+    shares,
     part_out,
     part_in,
     flat,
@@ -246,6 +247,10 @@
     attend(1 - side, True)
     pl.semaphore_wait(barrier, n - 1 + n_head - 1)
 
+    @pl.loop(0, half)
+    def _(i):
+        stat_copy((1 - side) * half + lax.rem(place + i, half)).start()
+
     @pl.loop(0, pairs)
     def _(i):
         pair = pair_at(1 - side, i)
@@ -253,12 +258,15 @@
         project(1 - side, 2 * pair * own, 2 * own)
         for t in (2 * pair, 2 * pair + 1):
             part_copy(t).start()
-            stat_copy(t).start()
 
     w_copy(side).start()
     w_copy(1 - side).start()
     near_queries().wait()
     attend(side, False)
+
+    @pl.loop(1, half)
+    def _(i):
+        stat_copy(near(i)).start()
 
     @pl.loop(0, pairs - 1)
     def _(i):
@@ -267,13 +275,11 @@
         project(side, 2 * pair * own, 2 * own)
         for t in (2 * pair, 2 * pair + 1):
             part_copy(t).start()
-            stat_copy(t).start()
 
     beside = me // 2 * 2 + 1 - lax.rem(me, 2)
     v_copy(me // 2).wait()
     project(side, beside * own, own)
     part_copy(beside).start()
-    stat_copy(beside).start()
     project(side, me * own, own)
     part_in[me] = part_out[me]
     stat_in[me] = stat_out[me]
@@ -286,13 +292,15 @@
     for d in range(n):
         spread[d * own : (d + 1) * own, :] = got[d] * scale
     share = jnp.transpose(spread[...])[:rows]
+    for at in range(n * own):
+        shares[at] = jnp.broadcast_to(share[:, at : at + 1], (rows, vdim))
 
     several(part_in, n - 1, part_send, part_recv).wait_recv()
     for j in range(own):
         y = jnp.zeros((rows, vdim), jnp.float32)
         for d in range(n):
             at = d * own + j
-            y = y + share[:, at : at + 1] * part_in[d, j].astype(jnp.float32)
+            y = y + shares[at] * part_in[d, j].astype(jnp.float32)
         flat[me, :, j * vdim : (j + 1) * vdim] = y.astype(jnp.bfloat16)
 
     flat_copy(mirror, me, 0).start()
@@ -376,6 +384,7 @@
             pltpu.VMEM((n, own, 128), jnp.float32),
             pltpu.VMEM((n, own, 128), jnp.float32),
             pltpu.VMEM((heads, 128), jnp.float32),
+            pltpu.VMEM((heads, rows, vdim), jnp.float32),
             pltpu.VMEM((n, own, rows, vdim), jnp.bfloat16),
             pltpu.VMEM((n, own, rows, vdim), jnp.bfloat16),
             pltpu.VMEM((n, rows, own * vdim), jnp.bfloat16),

time: 26.6 us -> 26.1 us (0.981)
  Pallas kernels: 25 us -> 24.6 us
    pallas_call x1, Pallas kernels: 25 us -> 24.6 us  [fused(): pl.pallas_call(functools.partial(kernel, n, n_head), out_shape=jax.ShapeD...]
where the time goes in v9:
time: 26.1 us; the launch traced here: 25.9 us
  Pallas kernels  24.6 us (94%)
  other arithmetic  1.38 us (5%)
    pallas_call x1, Pallas kernels, fused(): pl.pallas_call(functools.partial(kernel, n, n_head), out_shape=jax.ShapeD...  24.6 us
    reduce_sum x1, other arithmetic, fused(): return jnp.sum(groups.astype(jnp.float32), axis=0).astype(jnp.bfloat16)  1.38 us

profile of v9, /device:TPU:0, one launch (start us, length us, event | category | flops | bytes accessed | tf_op | source)
XLA Modules:
  0.0 25.9 jit_solution(10107165459366451914)
XLA Ops:
  0.0 24.6 %shard_map.64 = bf16[2,16,448]{2,1,0:T(8,128)(2,1)} custom-call(s32[16]{0:T(128)} %lengths_hbm.1, s32[16,32]{1,0:T(8,128)} %ids_hbm.1, bf16[16,64,576]{2,1,0:T(8,128)(2,1)} %q_hbm.1, bf16[16,576,128]{2,1,0:T(8,128)(2,1)} %bitcast.3, bf16[64,512,128]{2,1,0:T(8,128)(2,1)} %v_hbm.1, bf16[448,8192]{1,0:T(8,128)(2,1)} %bitcast.2), custom_call_target="tpu_custom_call" | custom-call | tf_op jit(solution)/shard_map/pallas_call | solution.py:370
  24.6 1.4 %reduce_sum.12 = bf16[16,448]{1,0:T(8,128)(2,1)} reduce(bf16[2,16,448]{2,1,0:T(8,128)(2,1)} %shard_map.64, bf16[]{:T(256)} %constant.2.clone.1), dimensions={0}, to_apply=%region_0.0 | reduce | flops 7168 | bytes 43010 | tf_op jit(solution)/shard_map/reduce_sum | solution.py:416
